TPU v7x, 128 devices: a whole 4x4x4 slice. The times are simulated.
128 devices in a mesh: stn: 32 (over y_lo, z, x), tm: 4 (over y_hi, core).
Axes of the slice: x: 4, y: 4 (y_hi: 2, y_lo: 2; y = y_hi * 2 + y_lo), z: 4, core: 2. Of those that a mesh axis runs over, the one named last changes fastest.
Arguments:
- voltages: bfloat16 [512, 4, 11, 2048], P('stn', 'tm'), may hold values from -6 to 6
- pfb_taps: float32 [4, 2048], replicated, may hold values from -3 to 3
- grid_kernel: float32 [8, 8], replicated, may hold values from 0.25 to 1
- uv_corners: int32 [32, 4, 34, 2, 256], P('stn', 'tm'), may hold values from 0 to 24
- kernel_offsets: int32 [32, 4, 34, 2, 256], P('stn', 'tm'), may hold values from 0 to 7
- row_counts: int32 [32, 4, 34], P('stn', 'tm'), may hold values from 128 to 256, as said below
- grid_tiles: int32 [32, 4, 34], P('stn', 'tm'), may hold values from 0 to 31, as said below
Outputs:
- uv_grid: float32 [32, 1024, 8, 256], P('stn', None, 'tm')
Inputs may be any that keep to these rules, and one draw needn't show every extreme that they name: `uv_corners`: each tile's kernel footprint of 8 cells along each direction lies inside its grid tile of 32 cells. `row_counts`: rows of a tile at or beyond its count are flagged. Every group and channel share has a tile with all 256 rows live and a tile with half of them live. `grid_tiles`: at most 2 tiles of one group and channel share name the same grid tile; in every draw some grid tile is named exactly 2 times by every group and channel share.
All inputs are finite; a program needn't handle non-finite values.
Results may differ from a plain program's by a relative error of at most 0.0072.
Values may be sent and summed in bfloat16 or wider, within the bound.
A program may use at most 128 MiB of HBM per device.

v0:
```python
import math

import jax
import jax.numpy as jnp
from jax import lax
from jax.sharding import PartitionSpec as P

CHANNELS = 1024
FRAME = 2048
TAPS = 4
BLOCK_CH = 128
ROWS = 256
SIDE = 32
CELLS = 1024
MOST = 2


def passed_along(block, axis, distance):
    devices = range(lax.axis_size(axis))
    route = [((i - distance) % len(devices), i) for i in devices]
    return lax.ppermute(block, axis, route)


def polyphase(voltages, filter_taps):
    frames = voltages.shape[1] - TAPS + 1
    filtered = jnp.zeros((voltages.shape[0], frames, voltages.shape[2]), jnp.float32)
    for tap_index in range(TAPS):
        filtered = filtered + filter_taps[tap_index][None, None, :] * voltages[
            :, tap_index : tap_index + frames, :
        ].astype(jnp.float32)
    return filtered.astype(jnp.bfloat16)


def transform_block(first_chan, block_width):
    samples = jnp.arange(FRAME, dtype=jnp.int32)
    channel_ids = first_chan + jnp.arange(block_width, dtype=jnp.int32)
    phase_int = samples[:, None] * channel_ids[None, :] % FRAME
    angle_rad = phase_int.astype(jnp.float32) * (2.0 * math.pi / FRAME)
    norm_scale = 1.0 / math.sqrt(FRAME)
    return (
        (jnp.cos(angle_rad) * norm_scale).astype(jnp.bfloat16),
        (-jnp.sin(angle_rad) * norm_scale).astype(jnp.bfloat16),
    )


def correlate(local_block, other_block):
    frames = local_block.shape[1]
    product = jnp.einsum(
        "atpc,btqc->cpaqb", local_block, other_block, preferred_element_type=jnp.float32
    )
    real_part = product[:, 0, :, 0, :] + product[:, 1, :, 1, :]
    imag_part = product[:, 1, :, 0, :] - product[:, 0, :, 1, :]
    visibility = jnp.stack([real_part, imag_part], axis=1) * (1.0 / frames)
    chan_count = visibility.shape[0]
    visibility = visibility.reshape(chan_count // BLOCK_CH, BLOCK_CH, 2, ROWS)
    visibility = jnp.transpose(visibility, (0, 3, 2, 1))
    return visibility.reshape(chan_count // BLOCK_CH, ROWS, 2 * BLOCK_CH).astype(jnp.bfloat16)


def tile_weights(corners, offsets, row_count, kernel):
    choose = offsets[:, :, None] == jnp.arange(kernel.shape[0], dtype=jnp.int32)[None, None, :]
    kern_rows = jnp.sum(jnp.where(choose[:, :, :, None], kernel[None, None, :, :], 0.0), axis=2)
    places = jnp.arange(SIDE, dtype=jnp.int32)
    reach_at = jnp.arange(kernel.shape[1], dtype=jnp.int32)
    hit_mask = (
        places[None, None, :, None] == corners[:, :, None, None] + reach_at[None, None, None, :]
    )
    axis_weight = jnp.sum(jnp.where(hit_mask, kern_rows[:, :, None, :], 0.0), axis=3)
    live_rows = (jnp.arange(corners.shape[1], dtype=jnp.int32) < row_count).astype(jnp.float32)
    weights = axis_weight[1][:, :, None] * axis_weight[0][:, None, :] * live_rows[:, None, None]
    return weights.reshape(corners.shape[1], SIDE * SIDE).astype(jnp.bfloat16)


def on_device(voltages, pfb_taps, grid_kernel, uv_corners, kernel_offsets, row_counts, grid_tiles):
    stations = voltages.shape[0]
    filtered = polyphase(voltages[:, 0], pfb_taps)
    frames_dev = filtered.shape[1]
    rows_in = filtered.reshape(stations * frames_dev, FRAME)
    block_width = min(256, CHANNELS)
    real_parts = []
    imag_parts = []
    for first_chan in range(0, CHANNELS, block_width):
        cos_part, sin_part = transform_block(first_chan, block_width)
        real_parts.append(jnp.dot(rows_in, cos_part, preferred_element_type=jnp.float32))
        imag_parts.append(jnp.dot(rows_in, sin_part, preferred_element_type=jnp.float32))
    spectra = jnp.stack(
        [jnp.concatenate(real_parts, axis=1), jnp.concatenate(imag_parts, axis=1)], axis=1
    )
    spectra = spectra.astype(jnp.bfloat16).reshape(stations, frames_dev, 2, CHANNELS)
    local_block = lax.all_to_all(spectra, "tm", split_axis=3, concat_axis=1, tiled=True)
    half_loop = lax.axis_size("stn") // 2
    own_tiles = correlate(local_block, local_block)

    def step_on(carried, unused):
        carried = passed_along(carried, "stn", -1)
        return (carried, correlate(local_block, carried))

    unused_last, distant = lax.scan(step_on, local_block, None, length=half_loop)
    vis_tiles = jnp.concatenate([own_tiles[None], distant], axis=0)
    ch_blocks = vis_tiles.shape[1]
    vis_tiles = vis_tiles.reshape(-1, ROWS, 2 * BLOCK_CH)
    tile_count = vis_tiles.shape[0]
    owners = grid_tiles[0, 0]
    tile_lists = jnp.concatenate([uv_corners[0, 0], kernel_offsets[0, 0]], axis=1).reshape(
        tile_count, 4 * ROWS
    )
    counts = row_counts[0, 0]
    blocks_of = jnp.arange(tile_count, dtype=jnp.int32) % ch_blocks
    same_owner = owners[:, None] == owners[None, :]
    tile_ids = jnp.arange(tile_count, dtype=jnp.int32)
    earlier = tile_ids[None, :] < tile_ids[:, None]
    slot_of = jnp.sum((same_owner & earlier).astype(jnp.int32), axis=1)
    peer_count = lax.axis_size("stn")
    chosen = (owners[:, None, None] == jnp.arange(peer_count, dtype=jnp.int32)[None, :, None]) & (
        slot_of[:, None, None] == jnp.arange(MOST, dtype=jnp.int32)[None, None, :]
    )
    send_vis = jnp.einsum(
        "kom,krc->omrc", chosen.astype(jnp.bfloat16), vis_tiles, preferred_element_type=jnp.float32
    ).astype(jnp.bfloat16)
    picker = chosen.astype(jnp.int32)
    send_lists = jnp.einsum("kom,kx->omx", picker, tile_lists)
    send_info = jnp.einsum("kom,kx->omx", picker, jnp.stack([counts, blocks_of], axis=1))
    slot_vis = lax.all_to_all(send_vis, "stn", split_axis=0, concat_axis=0, tiled=True)
    slot_lists = lax.all_to_all(send_lists, "stn", split_axis=0, concat_axis=0, tiled=True)
    slot_info = lax.all_to_all(send_info, "stn", split_axis=0, concat_axis=0, tiled=True)
    sources = slot_vis.shape[0]
    item_count = slot_vis.shape[1]
    group_size = 4
    rounds = sources // group_size
    vis_rounds = slot_vis.reshape(rounds, group_size, item_count, ROWS, 2 * BLOCK_CH)
    list_rounds = slot_lists.reshape(rounds, group_size, item_count, 4, ROWS)
    info_rounds = slot_info.reshape(rounds, group_size, item_count, 2)
    weigh_all = jax.vmap(jax.vmap(tile_weights, (0, 0, 0, None)), (0, 0, 0, None))

    def accumulate(running, packed):
        part_vis, part_lists, part_info = packed
        weights = weigh_all(
            part_lists[:, :, :2], part_lists[:, :, 2:], part_info[:, :, 0], grid_kernel
        )
        slot_terms = jnp.einsum(
            "girx,girc->gixc", weights, part_vis, preferred_element_type=jnp.float32
        )
        block_pick = (
            part_info[:, :, 1][:, :, None] == jnp.arange(ch_blocks, dtype=jnp.int32)[None, None, :]
        ).astype(jnp.float32)
        running = running + jnp.sum(
            block_pick[:, :, None, :, None] * slot_terms[:, :, :, None, :], axis=0
        )
        return (running, None)

    initial = jnp.zeros((item_count, CELLS, ch_blocks, 2 * BLOCK_CH), jnp.float32)
    result, unused_ys = lax.scan(accumulate, initial, (vis_rounds, list_rounds, info_rounds))
    gridded = jnp.sum(result, axis=0)
    return gridded[None]


def solution(mesh):
    return jax.shard_map(
        on_device,
        mesh=mesh,
        in_specs=(
            P("stn", "tm", None, None),
            P(),
            P(),
            P("stn", "tm", None, None, None),
            P("stn", "tm", None, None, None),
            P("stn", "tm", None),
            P("stn", "tm", None),
        ),
        out_specs=P("stn", None, "tm", None),
        check_vma=False,
    )
```

profile of v0, /device:TPU:8, one launch (start us, length us, event | category | flops | bytes accessed | tf_op | source)
XLA Modules:
  0.0 1005.5 jit_solution(17994992499544889380)
XLA Ops:
  3.0 8.1 convolution_convert_fusion.8
  11.1 8.1 convolution_convert_fusion.5
  19.2 8.3 convolution_convert_fusion.1
  27.6 8.1 convolution_convert_fusion.6
  35.6 8.5 convolution_convert_fusion.2
  44.2 8.1 convolution_convert_fusion.7
  52.3 8.3 convolution_convert_fusion.3
  60.6 8.1 convolution_convert_fusion.4
  90.3 7.8 all-to-all-done.2
  98.2 9.4 all-to-all-start
  127.4 7.4 convolution_bitcast_fusion.1
  140.1 487.7 %while.23 = (s32[]{:T(128)}, bf16[16,32,2,256]{3,1,2,0:T(8,128)(2,1)S(1)}, bf16[16,2,256,256]{3,2,1,0:T(8,128)(2,1)}, bf16[16,32,2,256]{1,0,2,3:T(8,128)(2,1)}, s32[]{:T(128)}) while((s32[]{:T(128)}, bf16[16,32,2,256]{3,1,2,0:T(8,128)(2,1)S(1)}, bf16[16,2,256,256]{3,2,1,0:T(8,128)(2,1)}, bf16[16,32,2,256]{1,0,2,3:T(8,128)(2,1)}, ...), condition=%wide.region_2.3_spmd, body=%wide.region_1.2_spmd.sunk | while | flops 17301504 | bytes 11272305 | solution.py:98
  145.4 10.4 %collective-permute-done = bf16[16,32,2,256]{3,1,2,0:T(8,128)(2,1)S(1)} collective-permute-done((bf16[16,32,2,256]{3,1,2,0:T(8,128)(2,1)S(1)}, bf16[16,32,2,256]{3,1,2,0:T(8,128)(2,1)S(1)}, u32[]{:S(2)}, u32[]{:S(2)}) %collective-permute-start) | collective-permute-done | bytes 524320 | tf_op jit(solution)/shard_map/while/body/eval_jaxpr/ppermute | solution.py:21
  158.8 7.4 convolution_bitcast_fusion.3
  179.1 9.5 collective-permute-done
  191.6 7.4 convolution_bitcast_fusion.3
  205.1 6.8 collective-permute-start
  211.9 8.6 collective-permute-done
  223.4 7.4 convolution_bitcast_fusion.3
  243.7 7.6 collective-permute-done
  254.4 7.4 convolution_bitcast_fusion.3
  284.4 7.4 convolution_bitcast_fusion.3
  314.4 7.4 convolution_bitcast_fusion.3
  344.3 7.4 convolution_bitcast_fusion.3
  374.3 7.4 convolution_bitcast_fusion.3
  404.3 7.4 convolution_bitcast_fusion.3
  434.3 7.4 convolution_bitcast_fusion.3
  447.8 6.8 collective-permute-start
  464.3 7.4 convolution_bitcast_fusion.3
  494.3 7.4 convolution_bitcast_fusion.3
  524.3 7.4 convolution_bitcast_fusion.3
  554.3 7.4 convolution_bitcast_fusion.3
  584.3 7.4 convolution_bitcast_fusion.3
  614.3 7.4 convolution_bitcast_fusion.3
  632.4 10.0 all-to-all-start.1
  642.4 9.7 convolution_convert_fusion
  652.1 11.4 %copy.151 = bf16[32,2,256,256]{3,2,1,0:T(8,128)(2,1)} copy(bf16[32,2,256,256]{3,0,2,1:T(8,128)(2,1)} %convolution_convert_fusion) | data formatting | bytes 16777216 | tf_op jit(solution)/shard_map/convert_element_type | solution.py:119
  663.5 8.9 all-to-all-start.3
  672.8 94.4 %all-to-all-done.3 = bf16[32,2,256,256]{3,2,1,0:T(8,128)(2,1)} async-done(((bf16[32,2,256,256]{3,2,1,0:T(8,128)(2,1)}), bf16[32,2,256,256]{3,2,1,0:T(8,128)(2,1)}, u32[]{:S(2)}, u32[]{:S(2)}) %all-to-all-start.3) | async-done | bytes 8388640 | tf_op jit(solution)/shard_map/all_to_all | solution.py:123
  767.2 232.4 %while.24 = (s32[]{:T(128)}, f32[2,1024,2,256]{3,1,2,0:T(8,128)}, s32[8,4,2,2]{1,3,2,0:T(2,128)S(1)}, s32[8,4,2,4,256]{4,3,2,1,0:T(4,128)S(1)}, f32[8,8]{1,0:T(8...) while((s32[]{:T(128)}, f32[2,1024,2,256]{3,1,2,0:T(8,128)}, ...), condition=%wide.region_7.8_spmd.clone, body=%wide.region_3.7_spmd.clone.sunk | while | flops 1093046272 | bytes 62637476 | solution.py:152
  783.4 7.0 multiply_reduce_fusion.2
  811.4 7.0 multiply_reduce_fusion.2
  840.6 7.0 multiply_reduce_fusion.2
  869.8 7.0 multiply_reduce_fusion.2
  899.0 7.0 multiply_reduce_fusion.2
  928.2 7.0 multiply_reduce_fusion.2
  957.4 7.0 multiply_reduce_fusion.2
  986.6 7.0 multiply_reduce_fusion.2
  (360 shorter events, 553.3 us)
Async XLA Ops:
  77.4 10.4 %copy-start.3 = (s32[1,1,34]{2,1,0:T(1,128)S(1)}, s32[1,1,34]{2,1,0:T(1,128)}, u32[]{:S(2)}) copy-start(s32[1,1,34]{2,1,0:T(1,128)} %param.17) | copy-start | bytes 412
  77.4 10.6 %copy-start.1 = (s32[1,1,34,2,256]{4,3,2,1,0:T(2,128)S(1)}, s32[1,1,34,2,256]{4,3,2,1,0:T(2,128)}, u32[]{:S(2)}) copy-start(s32[1,1,34,2,256]{4,3,2,1,0:T(2,128)} %param.15) | copy-start | bytes 208900
  77.4 10.6 %copy-start.2 = (s32[1,1,34,2,256]{4,3,2,1,0:T(2,128)S(1)}, s32[1,1,34,2,256]{4,3,2,1,0:T(2,128)}, u32[]{:S(2)}) copy-start(s32[1,1,34,2,256]{4,3,2,1,0:T(2,128)} %param.14) | copy-start | bytes 208900
  83.9 5.5 copy-start.4
  83.9 14.2 %all-to-all-start.2 = ((bf16[4,2,32768]{2,1,0:T(2,128)(2,1)}), bf16[4,2,32768]{2,1,0:T(2,128)(2,1)S(1)}, u32[]{:S(2)}, u32[]{:S(2)}) async-start(bf16[4,2,32768]{2,1,0:T(2,128)(2,1)} %reshape.267), calls=%async_computation.2 | async-start | bytes 1048576 | tf_op jit(solution)/shard_map/all_to_all | solution.py:90
  98.2 534.2 %all-to-all-start = ((s32[32,2,2]{2,1,0:T(2,128)}), s32[32,2,2]{2,1,0:T(2,128)S(1)}, u32[]{:S(2)}, u32[]{:S(2)}) async-start(s32[32,2,2]{2,1,0:T(2,128)} %copy.134), calls=%async_computation | async-start | bytes 65536 | tf_op jit(solution)/shard_map/all_to_all | solution.py:125
  140.5 15.3 %collective-permute-start = (bf16[16,32,2,256]{3,1,2,0:T(8,128)(2,1)S(1)}, bf16[16,32,2,256]{3,1,2,0:T(8,128)(2,1)S(1)}, u32[]{:S(2)}, u32[]{:S(2)}) collective-permute-start(bf16[16,32,2,256]{3,1,2,0:T(8,128)(2,1)S(1)} %get-tuple-element.268), channel_id=1, source_target_pairs={{4,0},{8,4},{12,8},{16,12},{20,16},{24,20},{28,24},{32,28},{36,32}... | collective-permute-start | bytes 1572872 | tf_op jit(solution)/shard_map/while/body/eval_jaxpr/ppermute | solution.py:21
  172.3 16.3 %collective-permute-start = (bf16[16,32,2,256]{3,1,2,0:T(8,128)(2,1)S(1)}, bf16[16,32,2,256]{3,1,2,0:T(8,128)(2,1)S(1)}, u32[]{:S(2)}, u32[]{:S(2)}) collective-permute-start(bf16[16,32,2,256]{3,1,2,0:T(8,128)(2,1)S(1)} %get-tuple-element.268), channel_id=1, source_target_pairs={{4,0},{8,4},{12,8},{16,12},{20,16},{24,20},{28,24},{32,28},{36,32}... | collective-permute-start | bytes 1572872 | tf_op jit(solution)/shard_map/while/body/eval_jaxpr/ppermute | solution.py:21
  205.1 15.3 %collective-permute-start = (bf16[16,32,2,256]{3,1,2,0:T(8,128)(2,1)S(1)}, bf16[16,32,2,256]{3,1,2,0:T(8,128)(2,1)S(1)}, u32[]{:S(2)}, u32[]{:S(2)}) collective-permute-start(bf16[16,32,2,256]{3,1,2,0:T(8,128)(2,1)S(1)} %get-tuple-element.268), channel_id=1, source_target_pairs={{4,0},{8,4},{12,8},{16,12},{20,16},{24,20},{28,24},{32,28},{36,32}... | collective-permute-start | bytes 1572872 | tf_op jit(solution)/shard_map/while/body/eval_jaxpr/ppermute | solution.py:21
  236.9 14.4 %collective-permute-start = (bf16[16,32,2,256]{3,1,2,0:T(8,128)(2,1)S(1)}, bf16[16,32,2,256]{3,1,2,0:T(8,128)(2,1)S(1)}, u32[]{:S(2)}, u32[]{:S(2)}) collective-permute-start(bf16[16,32,2,256]{3,1,2,0:T(8,128)(2,1)S(1)} %get-tuple-element.268), channel_id=1, source_target_pairs={{4,0},{8,4},{12,8},{16,12},{20,16},{24,20},{28,24},{32,28},{36,32}... | collective-permute-start | bytes 1572872 | tf_op jit(solution)/shard_map/while/body/eval_jaxpr/ppermute | solution.py:21
  267.9 13.5 %collective-permute-start = (bf16[16,32,2,256]{3,1,2,0:T(8,128)(2,1)S(1)}, bf16[16,32,2,256]{3,1,2,0:T(8,128)(2,1)S(1)}, u32[]{:S(2)}, u32[]{:S(2)}) collective-permute-start(bf16[16,32,2,256]{3,1,2,0:T(8,128)(2,1)S(1)} %get-tuple-element.268), channel_id=1, source_target_pairs={{4,0},{8,4},{12,8},{16,12},{20,16},{24,20},{28,24},{32,28},{36,32}... | collective-permute-start | bytes 1572872 | tf_op jit(solution)/shard_map/while/body/eval_jaxpr/ppermute | solution.py:21
  297.9 13.5 %collective-permute-start = (bf16[16,32,2,256]{3,1,2,0:T(8,128)(2,1)S(1)}, bf16[16,32,2,256]{3,1,2,0:T(8,128)(2,1)S(1)}, u32[]{:S(2)}, u32[]{:S(2)}) collective-permute-start(bf16[16,32,2,256]{3,1,2,0:T(8,128)(2,1)S(1)} %get-tuple-element.268), channel_id=1, source_target_pairs={{4,0},{8,4},{12,8},{16,12},{20,16},{24,20},{28,24},{32,28},{36,32}... | collective-permute-start | bytes 1572872 | tf_op jit(solution)/shard_map/while/body/eval_jaxpr/ppermute | solution.py:21
  327.9 13.5 %collective-permute-start = (bf16[16,32,2,256]{3,1,2,0:T(8,128)(2,1)S(1)}, bf16[16,32,2,256]{3,1,2,0:T(8,128)(2,1)S(1)}, u32[]{:S(2)}, u32[]{:S(2)}) collective-permute-start(bf16[16,32,2,256]{3,1,2,0:T(8,128)(2,1)S(1)} %get-tuple-element.268), channel_id=1, source_target_pairs={{4,0},{8,4},{12,8},{16,12},{20,16},{24,20},{28,24},{32,28},{36,32}... | collective-permute-start | bytes 1572872 | tf_op jit(solution)/shard_map/while/body/eval_jaxpr/ppermute | solution.py:21
  357.9 13.5 %collective-permute-start = (bf16[16,32,2,256]{3,1,2,0:T(8,128)(2,1)S(1)}, bf16[16,32,2,256]{3,1,2,0:T(8,128)(2,1)S(1)}, u32[]{:S(2)}, u32[]{:S(2)}) collective-permute-start(bf16[16,32,2,256]{3,1,2,0:T(8,128)(2,1)S(1)} %get-tuple-element.268), channel_id=1, source_target_pairs={{4,0},{8,4},{12,8},{16,12},{20,16},{24,20},{28,24},{32,28},{36,32}... | collective-permute-start | bytes 1572872 | tf_op jit(solution)/shard_map/while/body/eval_jaxpr/ppermute | solution.py:21
  387.8 13.5 %collective-permute-start = (bf16[16,32,2,256]{3,1,2,0:T(8,128)(2,1)S(1)}, bf16[16,32,2,256]{3,1,2,0:T(8,128)(2,1)S(1)}, u32[]{:S(2)}, u32[]{:S(2)}) collective-permute-start(bf16[16,32,2,256]{3,1,2,0:T(8,128)(2,1)S(1)} %get-tuple-element.268), channel_id=1, source_target_pairs={{4,0},{8,4},{12,8},{16,12},{20,16},{24,20},{28,24},{32,28},{36,32}... | collective-permute-start | bytes 1572872 | tf_op jit(solution)/shard_map/while/body/eval_jaxpr/ppermute | solution.py:21
  417.8 13.5 %collective-permute-start = (bf16[16,32,2,256]{3,1,2,0:T(8,128)(2,1)S(1)}, bf16[16,32,2,256]{3,1,2,0:T(8,128)(2,1)S(1)}, u32[]{:S(2)}, u32[]{:S(2)}) collective-permute-start(bf16[16,32,2,256]{3,1,2,0:T(8,128)(2,1)S(1)} %get-tuple-element.268), channel_id=1, source_target_pairs={{4,0},{8,4},{12,8},{16,12},{20,16},{24,20},{28,24},{32,28},{36,32}... | collective-permute-start | bytes 1572872 | tf_op jit(solution)/shard_map/while/body/eval_jaxpr/ppermute | solution.py:21
  447.8 13.5 %collective-permute-start = (bf16[16,32,2,256]{3,1,2,0:T(8,128)(2,1)S(1)}, bf16[16,32,2,256]{3,1,2,0:T(8,128)(2,1)S(1)}, u32[]{:S(2)}, u32[]{:S(2)}) collective-permute-start(bf16[16,32,2,256]{3,1,2,0:T(8,128)(2,1)S(1)} %get-tuple-element.268), channel_id=1, source_target_pairs={{4,0},{8,4},{12,8},{16,12},{20,16},{24,20},{28,24},{32,28},{36,32}... | collective-permute-start | bytes 1572872 | tf_op jit(solution)/shard_map/while/body/eval_jaxpr/ppermute | solution.py:21
  477.8 13.5 %collective-permute-start = (bf16[16,32,2,256]{3,1,2,0:T(8,128)(2,1)S(1)}, bf16[16,32,2,256]{3,1,2,0:T(8,128)(2,1)S(1)}, u32[]{:S(2)}, u32[]{:S(2)}) collective-permute-start(bf16[16,32,2,256]{3,1,2,0:T(8,128)(2,1)S(1)} %get-tuple-element.268), channel_id=1, source_target_pairs={{4,0},{8,4},{12,8},{16,12},{20,16},{24,20},{28,24},{32,28},{36,32}... | collective-permute-start | bytes 1572872 | tf_op jit(solution)/shard_map/while/body/eval_jaxpr/ppermute | solution.py:21
  507.8 13.5 %collective-permute-start = (bf16[16,32,2,256]{3,1,2,0:T(8,128)(2,1)S(1)}, bf16[16,32,2,256]{3,1,2,0:T(8,128)(2,1)S(1)}, u32[]{:S(2)}, u32[]{:S(2)}) collective-permute-start(bf16[16,32,2,256]{3,1,2,0:T(8,128)(2,1)S(1)} %get-tuple-element.268), channel_id=1, source_target_pairs={{4,0},{8,4},{12,8},{16,12},{20,16},{24,20},{28,24},{32,28},{36,32}... | collective-permute-start | bytes 1572872 | tf_op jit(solution)/shard_map/while/body/eval_jaxpr/ppermute | solution.py:21
  537.8 13.5 %collective-permute-start = (bf16[16,32,2,256]{3,1,2,0:T(8,128)(2,1)S(1)}, bf16[16,32,2,256]{3,1,2,0:T(8,128)(2,1)S(1)}, u32[]{:S(2)}, u32[]{:S(2)}) collective-permute-start(bf16[16,32,2,256]{3,1,2,0:T(8,128)(2,1)S(1)} %get-tuple-element.268), channel_id=1, source_target_pairs={{4,0},{8,4},{12,8},{16,12},{20,16},{24,20},{28,24},{32,28},{36,32}... | collective-permute-start | bytes 1572872 | tf_op jit(solution)/shard_map/while/body/eval_jaxpr/ppermute | solution.py:21
  567.8 13.5 %collective-permute-start = (bf16[16,32,2,256]{3,1,2,0:T(8,128)(2,1)S(1)}, bf16[16,32,2,256]{3,1,2,0:T(8,128)(2,1)S(1)}, u32[]{:S(2)}, u32[]{:S(2)}) collective-permute-start(bf16[16,32,2,256]{3,1,2,0:T(8,128)(2,1)S(1)} %get-tuple-element.268), channel_id=1, source_target_pairs={{4,0},{8,4},{12,8},{16,12},{20,16},{24,20},{28,24},{32,28},{36,32}... | collective-permute-start | bytes 1572872 | tf_op jit(solution)/shard_map/while/body/eval_jaxpr/ppermute | solution.py:21
  597.8 13.5 %collective-permute-start = (bf16[16,32,2,256]{3,1,2,0:T(8,128)(2,1)S(1)}, bf16[16,32,2,256]{3,1,2,0:T(8,128)(2,1)S(1)}, u32[]{:S(2)}, u32[]{:S(2)}) collective-permute-start(bf16[16,32,2,256]{3,1,2,0:T(8,128)(2,1)S(1)} %get-tuple-element.268), channel_id=1, source_target_pairs={{4,0},{8,4},{12,8},{16,12},{20,16},{24,20},{28,24},{32,28},{36,32}... | collective-permute-start | bytes 1572872 | tf_op jit(solution)/shard_map/while/body/eval_jaxpr/ppermute | solution.py:21
  632.4 31.1 %all-to-all-start.1 = ((s32[32,2,1024]{2,1,0:T(2,128)}), s32[32,2,1024]{2,1,0:T(2,128)S(1)}, u32[]{:S(2)}, u32[]{:S(2)}) async-start(s32[32,2,1024]{2,1,0:T(2,128)} %copy.136), calls=%async_computation.1 | async-start | bytes 524288 | tf_op jit(solution)/shard_map/all_to_all | solution.py:124
  663.5 103.8 %copy-start = (f32[8,8]{1,0:T(8,128)S(1)}, f32[8,8]{1,0:T(8,128)}, u32[]{:S(2)}) copy-start(f32[8,8]{1,0:T(8,128)} %param.13) | copy-start | bytes 772
  663.5 103.8 %all-to-all-start.3 = ((bf16[32,2,256,256]{3,2,1,0:T(8,128)(2,1)}), bf16[32,2,256,256]{3,2,1,0:T(8,128)(2,1)}, u32[]{:S(2)}, u32[]{:S(2)}) async-start(bf16[32,2,256,256]{3,2,1,0:T(8,128)(2,1)} %copy.151), calls=%async_computation.3 | async-start | bytes 16777216 | tf_op jit(solution)/shard_map/all_to_all | solution.py:123
where the time goes:
time: 1020 us; the launch traced here: 1010 us
  matrix products  248 us (24%)
  other arithmetic  234 us (23%)
  waiting for transfers between devices  219 us (21%)
  local copies, waits for them, and re-layouts  164 us (16%)
  starting transfers between devices  139 us (14%)
    dot_general x17, matrix products, correlate(): jnp.einsum('atpc,btqc->cpaqb', local_block, other_block, preferred_elemen...  126 us
    ppermute x16, waiting for transfers between devices, passed_along(): return lax.ppermute(block, axis, route)  117 us
    ppermute x16, starting transfers between devices, passed_along(): return lax.ppermute(block, axis, route)  106 us
    all_to_all x1, waiting for transfers between devices, on_device(): lax.all_to_all(send_vis, 'stn', split_axis=0, concat_axis=0, tiled=True)  94.4 us
    reduce_sum x8, other arithmetic, accumulate(): jnp.sum(block_pick[:, :, None, :, None] * slot_terms[:, :, :, None, :], a...  56.4 us
    ppermute x16, local copies, waits for them, and re-layouts, passed_along(): return lax.ppermute(block, axis, route)  47.9 us
    add x8, other arithmetic, accumulate(): running + jnp.sum(block_pick[:, :, None, :, None] * slot_terms[:, :, :, N...  46.7 us
    dot_general x8, matrix products, accumulate(): jnp.einsum('girx,girc->gixc', weights, part_vis, preferred_element_type=j...  45.7 us
  transfers between devices with their start and end apart: 20, of which 18 were waited for; matrix products, arithmetic and copies ran while one was open for 32% of the time, Pallas kernels for 0%

commit v1 on v0

v1 whole, which is shorter than its diff:
```python
import math

import jax
import jax.numpy as jnp
import ml_dtypes
import numpy as np
from jax import lax
from jax.experimental import pallas as pl
from jax.experimental.pallas import tpu as pltpu
from jax.sharding import PartitionSpec as P

CHANNELS = 1024
FRAME = 2048
TAPS = 4
FR_DEV = 8
STN_DEV = 16
BLOCK_CH = 128
ROWS = 256
SIDE = 32
CELLS = 1024
MOST = 2
GROUPS = 32
SLOTS = GROUPS * MOST
LISTS = 4 * ROWS
BF = jnp.bfloat16
F32 = jnp.float32
MESH = pl.DeviceIdType.MESH

UNITS = 32
A0, A1 = 0, 11
B0, B1 = 11, 22
C10, C1M, C11 = 22, 25, 27
C20, C2M, C21 = 27, 29, 32
MESSAGES = 38


def dft_table():
    samples = np.arange(FRAME, dtype=np.int64)
    channels = np.arange(CHANNELS, dtype=np.int64)
    phase = (samples[:, None] * channels[None, :]) % FRAME
    angle = phase.astype(np.float32) * np.float32(2.0 * math.pi / FRAME)
    scale = np.float32(1.0 / math.sqrt(FRAME))
    parts = np.stack([np.cos(angle) * scale, -np.sin(angle) * scale], axis=1)
    parts = parts.reshape(FRAME, 2, 4, 2, BLOCK_CH).transpose(2, 0, 3, 1, 4)
    return parts.reshape(4, FRAME, 4 * BLOCK_CH).astype(ml_dtypes.bfloat16)


def gather_kernel(info, filtered, table, out, grp0, grp1, grp2, grp3, held, tab, rows32, vis, tab_sem, a2a_send, a2a_recv, send_sem, recv_sem, out_sem):
    grp = (grp0, grp1, grp2, grp3)
    me_s = lax.axis_index("stn")
    me_t = lax.axis_index("tm")
    y, z, x = me_s // 16, (me_s // 4) % 4, me_s % 4
    xp, xm = (x + 1) % 4, (x + 3) % 4
    zp, zm = (z + 1) % 4, (z + 3) % 4
    yn = 1 - y

    def at(yy, zz, xx):
        return yy * 16 + zz * 4 + xx

    to = {
        "xp": at(y, z, xp),
        "xm": at(y, z, xm),
        "zp": at(y, zp, x),
        "zm": at(y, zm, x),
        "y": at(yn, z, x),
    }
    chunk = [(me_t + k) % 4 for k in range(4)]

    table_copies = [
        pltpu.make_async_copy(table.at[chunk[k]], tab.at[k], tab_sem.at[k]) for k in range(4)
    ]
    for copy in table_copies:
        copy.start()

    barrier = pltpu.get_barrier_semaphore()
    for name in to:
        pl.semaphore_signal(barrier, inc=1, device_id={"stn": to[name]}, device_id_type=MESH)
    for k in range(1, 4):
        pl.semaphore_signal(barrier, inc=1, device_id={"tm": chunk[k]}, device_id_type=MESH)

    def message(k, number, where, dest):
        ref = grp[k].at[where]
        return pltpu.make_async_remote_copy(
            src_ref=ref,
            dst_ref=ref,
            send_sem=send_sem.at[k, number],
            recv_sem=recv_sem.at[k, number],
            device_id={"stn": to[dest]},
            device_id_type=MESH,
        )

    def span(lo, hi):
        return pl.ds(lo, hi - lo)

    full4 = pl.ds(0, 4)
    both = pl.ds(0, 2)

    def build(k):
        def msg(number, where, dest):
            return (number, message(k, number, where, dest))

        a, b = span(A0, A1), span(B0, B1)
        c1, c2, c = span(C10, C11), span(C20, C21), span(C10, C21)
        direct1 = [
            msg(1, (y, z, x, c1), "xp"),
            msg(2, (y, z, x, c1), "xm"),
            msg(5, (y, z, x, c2), "zp"),
            msg(6, (y, z, x, c2), "zm"),
            msg(0, (y, z, x, span(A0, B1)), "y"),
        ]
        fwd1 = [
            (1, msg(3, (y, z, xm, span(C10, C1M)), "xp")),
            (2, msg(4, (y, z, xp, span(C1M, C11)), "xm")),
            (5, msg(7, (y, zm, x, span(C20, C2M)), "zp")),
            (6, msg(8, (y, zp, x, span(C2M, C21)), "zm")),
        ]
        rest1 = [0, 3, 4, 7, 8]
        direct2 = [
            msg(9, (both, z, x, a), "xp"),
            msg(10, (both, z, x, a), "xm"),
            msg(13, (both, z, x, b), "zp"),
            msg(14, (both, z, x, b), "zm"),
            msg(17, (y, z, full4, c1), "zp"),
            msg(18, (y, z, full4, c1), "zm"),
            msg(21, (y, full4, x, c2), "xp"),
            msg(22, (y, full4, x, c2), "xm"),
        ]
        lo2, hi2 = pl.ds(0, 2), pl.ds(2, 2)
        fwd2 = [
            (9, msg(11, (0, z, xm, a), "xp")),
            (10, msg(12, (1, z, xp, a), "xm")),
            (13, msg(15, (0, zm, x, b), "zp")),
            (14, msg(16, (1, zp, x, b), "zm")),
            (17, msg(19, (y, zm, lo2, c1), "zp")),
            (18, msg(20, (y, zp, hi2, c1), "zm")),
            (21, msg(23, (y, lo2, xm, c2), "xp")),
            (22, msg(24, (y, hi2, xp, c2), "xm")),
        ]
        rest2 = [11, 12, 15, 16, 19, 20, 23, 24]
        direct3 = [
            msg(25, (0, z, full4, a), "zp"),
            msg(27, (1, z, full4, a), "zm"),
            msg(31, (0, full4, x, b), "xp"),
            msg(33, (1, full4, x, b), "xm"),
            msg(37, (y, full4, full4, c), "y"),
            msg(26, (1, z, full4, a), "zp"),
            msg(28, (0, z, full4, a), "zm"),
            msg(32, (1, full4, x, b), "xp"),
            msg(34, (0, full4, x, b), "xm"),
        ]
        fwd3 = [
            (25, msg(29, (0, zm, full4, a), "zp")),
            (27, msg(30, (1, zp, full4, a), "zm")),
            (31, msg(35, (0, full4, xm, b), "xp")),
            (33, msg(36, (1, full4, xp, b), "xm")),
        ]
        rest3 = [26, 28, 32, 34, 29, 30, 35, 36, 37]
        return {1: (direct1, fwd1, rest1), 2: (direct2, fwd2, rest2), 3: (direct3, fwd3, rest3)}

    plan = [build(k) for k in range(4)]
    by_number = []
    for k in range(4):
        found = {}
        for step in (1, 2, 3):
            direct, fwd, rest = plan[k][step]
            for number, copy in direct:
                found[number] = copy
            for unused, (number, copy) in fwd:
                found[number] = copy
        by_number.append(found)

    def direct(step, k):
        for unused, copy in plan[k][step][0]:
            copy.start()

    def forward(step, k):
        for arrived, (unused, copy) in plan[k][step][1]:
            by_number[k][arrived].wait_recv()
            copy.start()

    def finish(step, k):
        for number in plan[k][step][2]:
            by_number[k][number].wait_recv()

    def transform(k, store):
        table_copies[k].wait()
        spectra = jnp.dot(filtered[...], tab[k], preferred_element_type=F32).astype(BF)
        for m in range(2):
            for t in range(FR_DEV):
                for p in range(2):
                    column = (m * 2 + p) * BLOCK_CH
                    store(
                        m * 16 + t * 2 + p,
                        spectra[t * STN_DEV : (t + 1) * STN_DEV, column : column + BLOCK_CH],
                    )

    def store_own(unit, value):
        grp[0][y, z, x, unit] = value

    transform(0, store_own)
    pl.semaphore_wait(barrier, 8)
    direct(1, 0)

    exchange = []
    for k in range(1, 4):

        def store_held(unit, value, k=k):
            held[k - 1, unit] = value

        transform(k, store_held)
        copy = pltpu.make_async_remote_copy(
            src_ref=held.at[k - 1],
            dst_ref=grp[4 - k].at[y, z, x],
            send_sem=a2a_send.at[k],
            recv_sem=a2a_recv.at[k],
            device_id={"tm": chunk[k]},
            device_id_type=MESH,
        )
        copy.start()
        exchange.append(copy)

    def exchanged(k):
        pltpu.make_async_remote_copy(
            src_ref=held.at[0],
            dst_ref=grp[k].at[y, z, x],
            send_sem=a2a_send.at[4 - k],
            recv_sem=a2a_recv.at[4 - k],
            device_id={"tm": chunk[k]},
            device_id_type=MESH,
        ).wait_recv()

    def correlate(k, first, last):
        def slot(s, carry):
            g = s // MOST
            partner, m = info[s * 2], info[s * 2 + 1]
            units = pl.ds(m * 16, 16)
            own = grp[k][g // 16, (g // 4) % 4, g % 4, units]
            rows32[...] = own.reshape(256, BLOCK_CH).astype(F32)
            other = grp[k][partner // 16, (partner // 4) % 4, partner % 4, units]
            for a in range(STN_DEV):
                real, imag = [], []
                for t in range(FR_DEV):
                    r = t * 32 + a
                    a_r = jnp.broadcast_to(rows32[r : r + 1, :], (STN_DEV, BLOCK_CH)).astype(BF)
                    a_i = jnp.broadcast_to(
                        rows32[r + 16 : r + 17, :], (STN_DEV, BLOCK_CH)
                    ).astype(BF)
                    b_r, b_i = other[2 * t], other[2 * t + 1]
                    real += [a_r * b_r + a_i * b_i]
                    imag += [a_i * b_r - a_r * b_i]
                while len(real) > 1:
                    real = [real[i] + real[i + 1] for i in range(0, len(real), 2)]
                    imag = [imag[i] + imag[i + 1] for i in range(0, len(imag), 2)]
                rows = slice(a * STN_DEV, (a + 1) * STN_DEV)
                if k == 0:
                    vis[s, rows, :BLOCK_CH] = real[0]
                    vis[s, rows, BLOCK_CH:] = imag[0]
                else:
                    vis[s, rows, :BLOCK_CH] = vis[s, rows, :BLOCK_CH] + real[0]
                    vis[s, rows, BLOCK_CH:] = vis[s, rows, BLOCK_CH:] + imag[0]
            return carry

        lax.fori_loop(first, last, slot, 0)

    half = SLOTS // 2
    for stage in range(6):
        active = [(step, stage - step + 1) for step in (3, 2, 1) if 0 <= stage - step + 1 < 4]
        for step, k in active:
            if step == 1 and k == 0:
                continue
            if step == 1:
                exchanged(k)
            direct(step, k)
        if stage >= 3:
            correlate(stage - 3, 0, half)
        for step, k in active:
            forward(step, k)
        if stage >= 3:
            correlate(stage - 3, half, SLOTS)
        for step, k in active:
            finish(step, k)
    copies = []
    for i in range(4):
        part = pl.ds(i * (SLOTS // 4), SLOTS // 4)
        correlate(3, i * (SLOTS // 4), (i + 1) * (SLOTS // 4))
        copy = pltpu.make_async_copy(vis.at[part], out.at[part], out_sem.at[i])
        copy.start()
        copies.append(copy)
    for k in range(4):
        for number in range(MESSAGES):
            by_number[k][number].wait_send()
    for copy in exchange:
        copy.wait_send()
    for copy in copies:
        copy.wait()


def gather_and_correlate(info, filtered, table):
    return pl.pallas_call(
        gather_kernel,
        out_shape=jax.ShapeDtypeStruct((SLOTS, ROWS, 2 * BLOCK_CH), BF),
        in_specs=[
            pl.BlockSpec(memory_space=pltpu.SMEM),
            pl.BlockSpec(memory_space=pltpu.VMEM),
            pl.BlockSpec(memory_space=pl.ANY),
        ],
        out_specs=pl.BlockSpec(memory_space=pl.ANY),
        scratch_shapes=[
            *[pltpu.VMEM((2, 4, 4, UNITS, STN_DEV, BLOCK_CH), BF) for unused in range(4)],
            pltpu.VMEM((3, UNITS, STN_DEV, BLOCK_CH), BF),
            pltpu.VMEM((4, FRAME, 4 * BLOCK_CH), BF),
            pltpu.VMEM((256, BLOCK_CH), F32),
            pltpu.VMEM((SLOTS, ROWS, 2 * BLOCK_CH), BF),
            pltpu.SemaphoreType.DMA((4,)),
            pltpu.SemaphoreType.DMA((4,)),
            pltpu.SemaphoreType.DMA((4,)),
            pltpu.SemaphoreType.DMA((4, MESSAGES)),
            pltpu.SemaphoreType.DMA((4, MESSAGES)),
            pltpu.SemaphoreType.DMA((4,)),
        ],
        compiler_params=pltpu.CompilerParams(
            collective_id=0, has_side_effects=True, vmem_limit_bytes=48 * 2**20
        ),
        name="gather_correlate",
    )(info, filtered, table)


def grid_kernel_body(info, count, lists, kernel_t, vis, out, total, weights):
    total[...] = jnp.zeros_like(total)

    def axis_weight(position, offset):
        chosen = jnp.zeros((8, ROWS), F32)
        for o in range(8):
            column = jnp.broadcast_to(kernel_t[:, o : o + 1], (8, ROWS))
            chosen = jnp.where(jnp.broadcast_to(offset == o, (8, ROWS)), column, chosen)
        reach = lax.broadcasted_iota(jnp.int32, (SIDE, ROWS), 0) - jnp.broadcast_to(
            position, (SIDE, ROWS)
        )
        placed = jnp.zeros((SIDE, ROWS), F32)
        for k in range(8):
            placed = jnp.where(
                reach == k, jnp.broadcast_to(chosen[k : k + 1], (SIDE, ROWS)), placed
            )
        return placed

    def slot(s, carry):
        m = info[s * 2 + 1]
        rows = lists[s].astype(jnp.int32)
        along_x = axis_weight(rows[0:1], rows[2:3])
        along_y = axis_weight(rows[1:2], rows[3:4])
        live = lax.broadcasted_iota(jnp.int32, (SIDE, ROWS), 1) < count[s]
        along_y = jnp.where(live, along_y, 0.0)
        for v in range(SIDE):
            weights[v * SIDE : (v + 1) * SIDE] = (
                along_x * jnp.broadcast_to(along_y[v : v + 1], (SIDE, ROWS))
            ).astype(BF)
        total[m] += jnp.dot(weights[...], vis[s], preferred_element_type=F32)
        return carry

    lax.fori_loop(0, SLOTS, slot, 0)
    for m in range(2):
        out[:, m * 256 : (m + 1) * 256] = total[m] * (1.0 / 32.0)


def gridding(info, count, lists, kernel_t, vis):
    vmem = pl.BlockSpec(memory_space=pltpu.VMEM)
    smem = pl.BlockSpec(memory_space=pltpu.SMEM)
    return pl.pallas_call(
        grid_kernel_body,
        out_shape=jax.ShapeDtypeStruct((CELLS, 2 * 2 * BLOCK_CH), F32),
        in_specs=[smem, smem, vmem, vmem, vmem],
        out_specs=vmem,
        scratch_shapes=[
            pltpu.VMEM((2, CELLS, 2 * BLOCK_CH), F32),
            pltpu.VMEM((CELLS, ROWS), BF),
        ],
        compiler_params=pltpu.CompilerParams(vmem_limit_bytes=40 * 2**20),
        name="gridding",
    )(info, count, lists, kernel_t, vis)


def polyphase(voltages, filter_taps):
    by_frame = jnp.transpose(voltages, (1, 0, 2))
    frames = by_frame.shape[0] - TAPS + 1
    filtered = jnp.zeros((frames,) + by_frame.shape[1:], F32)
    for tap in range(TAPS):
        filtered = filtered + filter_taps[tap][None, None, :] * by_frame[
            tap : tap + frames
        ].astype(F32)
    return filtered.astype(BF).reshape(frames * by_frame.shape[1], FRAME)


def route(uv_corners, kernel_offsets, row_counts, grid_tiles):
    owners = grid_tiles[0, 0]
    tiles = owners.shape[0]
    tile_ids = jnp.arange(tiles, dtype=jnp.int32)
    extra = jnp.stack([row_counts[0, 0], tile_ids // 2, tile_ids % 2], axis=1)
    extra = jnp.pad(extra, ((0, 0), (0, 125)))
    packed = jnp.concatenate(
        [uv_corners[0, 0].reshape(tiles, 512), kernel_offsets[0, 0].reshape(tiles, 512), extra],
        axis=1,
    ).astype(BF)
    same = owners[:, None] == owners[None, :]
    earlier = tile_ids[None, :] < tile_ids[:, None]
    slot_of = jnp.sum((same & earlier).astype(jnp.int32), axis=1)
    target = owners * MOST + slot_of
    picker = (target[None, :] == jnp.arange(SLOTS, dtype=jnp.int32)[:, None]).astype(BF)
    send = jnp.dot(picker, packed, preferred_element_type=F32).astype(BF)
    send = send.reshape(GROUPS, MOST, LISTS + 128)
    got = lax.all_to_all(send, "stn", split_axis=0, concat_axis=0, tiled=True)
    got = got.reshape(SLOTS, LISTS + 128)
    facts = got[:, LISTS : LISTS + 3].astype(jnp.int32)
    group = jnp.arange(SLOTS, dtype=jnp.int32) // MOST
    partner = (group + facts[:, 1]) % GROUPS
    info = jnp.stack([partner, facts[:, 2]], axis=1).reshape(-1)
    return info, facts[:, 0], got[:, :LISTS].reshape(SLOTS, 4, ROWS).astype(F32)


def on_device(voltages, pfb_taps, grid_kernel, uv_corners, kernel_offsets, row_counts, grid_tiles):
    info, count, lists = route(uv_corners, kernel_offsets, row_counts, grid_tiles)
    filtered = polyphase(voltages[:, 0], pfb_taps)
    vis = gather_and_correlate(info, filtered, jnp.asarray(dft_table()))
    gridded = gridding(info, count, lists, grid_kernel.T, vis)
    return gridded.reshape(1, CELLS, 2, 2 * BLOCK_CH)


def solution(mesh):
    return jax.shard_map(
        on_device,
        mesh=mesh,
        in_specs=(
            P("stn", "tm", None, None),
            P(),
            P(),
            P("stn", "tm", None, None, None),
            P("stn", "tm", None, None, None),
            P("stn", "tm", None),
            P("stn", "tm", None),
        ),
        out_specs=P("stn", None, "tm", None),
        check_vma=False,
    )
```

time: 1020 us -> 170 us (0.17); the launches traced: 1010 us -> 168 us
  matrix products: 248 us -> 0.17 us
  other arithmetic: 234 us -> 6.55 us
  waiting for transfers between devices: 219 us -> 3.48 us
  local copies, waits for them, and re-layouts: 164 us -> 8.67 us
  Pallas kernels: 0 us -> 139 us
  starting transfers between devices: 139 us -> 9.39 us
    dot_general x36 -> x1, matrix products: 248 us -> 0.17 us  [route(): send = jnp.dot(picker, packed, preferred_element_type=F32).astype(BF)]
    pallas_call x0 -> x2, Pallas kernels: none -> 139 us  [the longest x1 114 us: gather_and_correlate(): pl.pallas_call(gather_kernel, out_shape=jax.ShapeDtypeStruct((SLOTS, ROWS...]
    ppermute x16 -> x0, waiting for transfers between devices: 117 us -> none  [passed_along(): return lax.ppermute(block, axis, route)]
    ppermute x16 -> x0, starting transfers between devices: 106 us -> none  [passed_along(): return lax.ppermute(block, axis, route)]
    all_to_all x4 -> x1, waiting for transfers between devices: 102 us -> 3.48 us  [route(): got = lax.all_to_all(send, 'stn', split_axis=0, concat_axis=0, tiled=True)]
    add x36 -> x1, other arithmetic: 78.7 us -> 0.67 us  [route(): target = owners * MOST + slot_of]
    reduce_sum x26 -> x1, other arithmetic: 71.5 us -> 0.91 us  [route(): slot_of = jnp.sum((same & earlier).astype(jnp.int32), axis=1)]
    ppermute x16 -> x0, local copies, waits for them, and re-layouts: 47.9 us -> none  [passed_along(): return lax.ppermute(block, axis, route)]
  transfers between devices with their start and end apart: 20 -> 1, of which waited for: 18 -> 1; matrix products, arithmetic and copies ran while one was open for 32% -> 2% of each run, Pallas kernels for 0% -> 0%
where the time goes in v1:
time: 170 us; the launch traced here: 168 us
  Pallas kernels  139 us (82%)
  starting transfers between devices  9.39 us (6%)
  local copies, waits for them, and re-layouts  8.67 us (5%)
  other arithmetic  6.55 us (4%)
  waiting for transfers between devices  3.48 us (2%)
    pallas_call x1, Pallas kernels, gather_and_correlate(): pl.pallas_call(gather_kernel, out_shape=jax.ShapeDtypeStruct((SLOTS, ROWS...  114 us
    pallas_call x1, Pallas kernels, gridding(): pl.pallas_call(grid_kernel_body, out_shape=jax.ShapeDtypeStruct((CELLS, 2...  25.6 us
    all_to_all x1, starting transfers between devices, route(): got = lax.all_to_all(send, 'stn', split_axis=0, concat_axis=0, tiled=True)  9.39 us
    unnamed x8, local copies, waits for them, and re-layouts  4.33 us
    all_to_all x1, waiting for transfers between devices, route(): got = lax.all_to_all(send, 'stn', split_axis=0, concat_axis=0, tiled=True)  3.48 us
  transfers between devices with their start and end apart: 1, of which 1 were waited for; matrix products, arithmetic and copies ran while one was open for 2% of the time, Pallas kernels for 0%

profile of v1, /device:TPU:8, one launch (start us, length us, event | category | flops | bytes accessed | tf_op | source)
XLA Modules:
  0.0 167.6 jit_solution(3195850305054080869)
XLA Ops:
  0.0 0.7 convert_bitcast_fusion.2
  0.7 0.9 convert_reduce_fusion
  1.6 0.7 multiply_add_fusion
  2.3 0.1 copy.25
  2.4 0.9 convert_bitcast_fusion.1
  3.3 0.9 convert_bitcast_fusion
  4.3 0.2 convolution_convert_fusion
  4.5 0.7 reshape.116
  5.2 9.4 %all-to-all-start = ((bf16[32,2,1152]{2,1,0:T(2,128)(2,1)}), bf16[32,2,1152]{2,1,0:T(2,128)(2,1)S(1)}, u32[]{:S(2)}, u32[]{:S(2)}) async-start(bf16[32,2,1152]{2,1,0:T(2,128)(2,1)} %reshape.116), calls=%async_computation | async-start | bytes 294912 | tf_op jit(solution)/shard_map/all_to_all | solution.py:410
  14.6 0.9 fusion.21
  15.6 2.2 %add_convert_fusion = bf16[8,16,2048]{2,1,0:T(8,128)(2,1)S(1)} fusion(bf16[11,16,2048]{2,1,0:T(8,128)(2,1)} %bitcast.25, f32[2048]{0:T(1024)S(1)} %bitcast.32, f32[2048]{0:T(1024)S(1)} %bitcast.33, f32[2048]{0:T(1024)S(1)} %bitcast.31, f32[2048]{0:T(1024)S(1)} %bitcast.30), kind=kLoop, calls=%fused_computation.1 | loop fusion | flops 3145728 | bytes 2654208 | tf_op jit(solution)/shard_map/convert_element_type | solution.py:390
  17.8 0.8 copy.24
  18.6 3.5 %all-to-all-done = bf16[32,2,1152]{2,1,0:T(2,128)(2,1)S(1)} async-done(((bf16[32,2,1152]{2,1,0:T(2,128)(2,1)}), bf16[32,2,1152]{2,1,0:T(2,128)(2,1)S(1)}, u32[]{:S(2)}, u32[]{:S(2)}) %all-to-all-start) | async-done | bytes 147488 | tf_op jit(solution)/shard_map/all_to_all | solution.py:410
  22.0 0.1 reshape.117
  22.2 0.1 slice_reduce_fusion
  22.3 0.1 pad_add_fusion
  22.4 0.1 reshape.118.info
  22.5 0.1 reshape.121.lists
  22.6 113.6 %gather_correlate.1.vis = bf16[64,256,256]{2,1,0:T(8,128)(2,1)} custom-call(s32[128]{0:T(128)S(1)} %reshape.118.info, bf16[128,2048]{1,0:T(8,128)(2,1)S(1)} %bitcast.23, bf16[4,2048,512]{2,1,0:T(8,128)(2,1)} %constant.60.clone.table), custom_call_target="tpu_custom_call" | custom-call | tf_op jit(solution)/shard_map/gather_correlate/pallas_call | solution.py:299
  136.2 0.0 copy-start
  136.2 3.4 %copy-done = bf16[64,256,256]{2,1,0:T(8,128)(2,1)S(1)} copy-done((bf16[64,256,256]{2,1,0:T(8,128)(2,1)S(1)}, bf16[64,256,256]{2,1,0:T(8,128)(2,1)}, u32[]{:S(2)}) %copy-start) | copy-done | bytes 8388632
  139.6 25.6 %gridding.1 = f32[1024,512]{1,0:T(8,128)S(1)} custom-call(s32[128]{0:T(128)S(1)} %reshape.118.info, s32[64]{0:T(128)S(1)} %get-tuple-element.9.count, f32[64,4,256]{2,1,0:T(4,128)S(1)} %reshape.121.lists, f32[8,8]{1,0:T(8,128)S(1)} %bitcast.24, bf16[64,256,256]{2,1,0:T(8,128)(2,1)S(1)} %copy-done), custom_call_target="tpu_custom_call" | custom-call | tf_op jit(solution)/shard_map/gridding/pallas_call | solution.py:368
  165.3 2.4 %reshape.120 = f32[1,1024,2,256]{3,2,1,0:T(2,128)} reshape(f32[1024,512]{1,0:T(8,128)S(1)} %gridding.1) | data formatting | bytes 4194304 | tf_op jit(solution)/shard_map/reshape | solution.py:424
  (8 shorter events, 0.1 us)
Async XLA Ops:
  5.2 16.8 %all-to-all-start = ((bf16[32,2,1152]{2,1,0:T(2,128)(2,1)}), bf16[32,2,1152]{2,1,0:T(2,128)(2,1)S(1)}, u32[]{:S(2)}, u32[]{:S(2)}) async-start(bf16[32,2,1152]{2,1,0:T(2,128)(2,1)} %reshape.116), calls=%async_computation | async-start | bytes 294912 | tf_op jit(solution)/shard_map/all_to_all | solution.py:410
  136.2 3.4 %copy-start = (bf16[64,256,256]{2,1,0:T(8,128)(2,1)S(1)}, bf16[64,256,256]{2,1,0:T(8,128)(2,1)}, u32[]{:S(2)}) copy-start(bf16[64,256,256]{2,1,0:T(8,128)(2,1)} %gather_correlate.1.vis) | copy-start | bytes 25165828

commit v2 on v1

--- a/solution.py
+++ b/solution.py
@@ -45,7 +45,38 @@
     return parts.reshape(4, FRAME, 4 * BLOCK_CH).astype(ml_dtypes.bfloat16)
 
 
-def gather_kernel(info, filtered, table, out, grp0, grp1, grp2, grp3, held, tab, rows32, vis, tab_sem, a2a_send, a2a_recv, send_sem, recv_sem, out_sem):
+def gather_kernel(
+    lists,
+    facts,
+    filtered,
+    table,
+    out,
+    out_lists,
+    out_facts,
+    grp0,
+    grp1,
+    grp2,
+    grp3,
+    held,
+    tab,
+    rows32,
+    vis,
+    to_send,
+    by_y,
+    by_z,
+    by_x,
+    facts_all,
+    info,
+    tab_sem,
+    a2a_send,
+    a2a_recv,
+    send_sem,
+    recv_sem,
+    out_sem,
+    route_send,
+    route_recv,
+    own_sem,
+):
     grp = (grp0, grp1, grp2, grp3)
     me_s = lax.axis_index("stn")
     me_t = lax.axis_index("tm")
@@ -64,17 +95,20 @@
         "zm": at(y, zm, x),
         "y": at(yn, z, x),
     }
+    along_z = [at(y, (z + i) % 4, x) for i in range(4)]
+    along_x = [at(y, z, (x + i) % 4) for i in range(4)]
     chunk = [(me_t + k) % 4 for k in range(4)]
 
     table_copies = [
         pltpu.make_async_copy(table.at[chunk[k]], tab.at[k], tab_sem.at[k]) for k in range(4)
     ]
-    for copy in table_copies:
-        copy.start()
+    table_copies[0].start()
 
     barrier = pltpu.get_barrier_semaphore()
     for name in to:
         pl.semaphore_signal(barrier, inc=1, device_id={"stn": to[name]}, device_id_type=MESH)
+    for far in (along_z[2], along_x[2]):
+        pl.semaphore_signal(barrier, inc=1, device_id={"stn": far}, device_id_type=MESH)
     for k in range(1, 4):
         pl.semaphore_signal(barrier, inc=1, device_id={"tm": chunk[k]}, device_id_type=MESH)
 
@@ -184,6 +218,9 @@
 
     def transform(k, store):
         table_copies[k].wait()
+        if k == 0:
+            for copy in table_copies[1:]:
+                copy.start()
         spectra = jnp.dot(filtered[...], tab[k], preferred_element_type=F32).astype(BF)
         for m in range(2):
             for t in range(FR_DEV):
@@ -197,14 +234,33 @@
     def store_own(unit, value):
         grp[0][y, z, x, unit] = value
 
-    transform(0, store_own)
-    pl.semaphore_wait(barrier, 8)
-    direct(1, 0)
-
+    for dest in range(GROUPS):
+        place = (dest // 16, (dest // 4) % 4, dest % 4)
+        to_send[place + (0,)] = lists[dest]
+        to_send[place + (1,)] = jnp.concatenate(
+            [jnp.broadcast_to(facts[i : i + 1], (8, BLOCK_CH)) for i in (dest * 2, dest * 2 + 1)],
+            axis=0,
+        ).astype(BF)
+
+    def route(number, source, target, device):
+        return pltpu.make_async_remote_copy(
+            src_ref=source,
+            dst_ref=target,
+            send_sem=route_send.at[number],
+            recv_sem=route_recv.at[number],
+            device_id={"stn": device},
+            device_id_type=MESH,
+        )
+
+    pl.semaphore_wait(barrier, 10)
+    route_y = route(0, to_send.at[yn], by_y.at[y], to["y"])
+    route_y.start()
+    keep_y = pltpu.make_async_copy(to_send.at[y], by_y.at[y], own_sem.at[0])
+    keep_y.start()
     exchange = []
-    for k in range(1, 4):
-
-        def store_held(unit, value, k=k):
+
+    def exchange_out(k):
+        def store_held(unit, value):
             held[k - 1, unit] = value
 
         transform(k, store_held)
@@ -232,7 +288,8 @@
     def correlate(k, first, last):
         def slot(s, carry):
             g = s // MOST
-            partner, m = info[s * 2], info[s * 2 + 1]
+            partner = jnp.clip(info[s, 1], 0, GROUPS - 1)
+            m = jnp.clip(info[s, 2], 0, 1)
             units = pl.ds(m * 16, 16)
             own = grp[k][g // 16, (g // 4) % 4, g % 4, units]
             rows32[...] = own.reshape(256, BLOCK_CH).astype(F32)
@@ -262,23 +319,78 @@
 
         lax.fori_loop(first, last, slot, 0)
 
+    transform(0, store_own)
+    direct(1, 0)
+    keep_y.wait()
+    route_y.wait_recv()
+    routes_z = [
+        route(i, by_y.at[:, (z + i) % 4], by_z.at[z], along_z[i]) for i in range(1, 4)
+    ]
+    for copy in routes_z:
+        copy.start()
+    keep_z = pltpu.make_async_copy(by_y.at[:, z], by_z.at[z], own_sem.at[1])
+    keep_z.start()
+    exchange_out(1)
+    forward(1, 0)
+    exchange_out(2)
+    finish(1, 0)
+    direct(2, 0)
+    keep_z.wait()
+    for copy in routes_z:
+        copy.wait_recv()
+    routes_x = [
+        route(3 + i, by_z.at[:, :, (x + i) % 4], by_x.at[x], along_x[i]) for i in range(1, 4)
+    ]
+    for copy in routes_x:
+        copy.start()
+    keep_x = pltpu.make_async_copy(by_z.at[:, :, x], by_x.at[x], own_sem.at[2])
+    keep_x.start()
+    exchange_out(3)
+    forward(2, 0)
+    exchanged(1)
+    direct(1, 1)
+    exchanged(2)
+    direct(1, 2)
+    forward(1, 1)
+    finish(1, 1)
+    direct(2, 1)
+    finish(2, 0)
+    direct(3, 0)
+    exchanged(3)
+    direct(1, 3)
+    forward(1, 2)
+    forward(1, 3)
+    keep_x.wait()
+    for copy in routes_x:
+        copy.wait_recv()
+    for g in range(GROUPS):
+        unit = by_x[g % 4, (g // 4) % 4, g // 16, 1].astype(F32).astype(jnp.int32)
+        facts_all[2 * g : 2 * g + 1] = unit[0:1]
+        facts_all[2 * g + 1 : 2 * g + 2] = unit[8:9]
+    to_scalars = pltpu.make_async_copy(facts_all, info, own_sem.at[3])
+    to_scalars.start()
+    to_next = pltpu.make_async_copy(facts_all, out_facts, own_sem.at[4])
+    to_next.start()
+    lists_next = pltpu.make_async_copy(by_x, out_lists, own_sem.at[5])
+    lists_next.start()
+    to_scalars.wait()
+    forward(2, 1)
     half = SLOTS // 2
-    for stage in range(6):
-        active = [(step, stage - step + 1) for step in (3, 2, 1) if 0 <= stage - step + 1 < 4]
-        for step, k in active:
-            if step == 1 and k == 0:
-                continue
-            if step == 1:
-                exchanged(k)
-            direct(step, k)
-        if stage >= 3:
-            correlate(stage - 3, 0, half)
-        for step, k in active:
-            forward(step, k)
-        if stage >= 3:
-            correlate(stage - 3, half, SLOTS)
-        for step, k in active:
-            finish(step, k)
+    for k in range(4):
+        if k < 2:
+            finish(1, k + 2)
+            direct(2, k + 2)
+        forward(3, k)
+        if k > 0:
+            correlate(k - 1, half, SLOTS)
+        if k < 3:
+            finish(2, k + 1)
+            direct(3, k + 1)
+        if k < 2:
+            forward(2, k + 2)
+        finish(3, k)
+        if k < 3:
+            correlate(k, 0, half)
     copies = []
     for i in range(4):
         part = pl.ds(i * (SLOTS // 4), SLOTS // 4)
@@ -293,40 +405,121 @@
         copy.wait_send()
     for copy in copies:
         copy.wait()
-
-
-def gather_and_correlate(info, filtered, table):
+    for copy in [route_y] + routes_z + routes_x:
+        copy.wait_send()
+    to_next.wait()
+    lists_next.wait()
+
+
+def gather_and_correlate(lists, facts, filtered, table):
+    vmem = pl.BlockSpec(memory_space=pltpu.VMEM)
+    anywhere = pl.BlockSpec(memory_space=pl.ANY)
     return pl.pallas_call(
         gather_kernel,
-        out_shape=jax.ShapeDtypeStruct((SLOTS, ROWS, 2 * BLOCK_CH), BF),
-        in_specs=[
-            pl.BlockSpec(memory_space=pltpu.SMEM),
-            pl.BlockSpec(memory_space=pltpu.VMEM),
-            pl.BlockSpec(memory_space=pl.ANY),
-        ],
-        out_specs=pl.BlockSpec(memory_space=pl.ANY),
+        out_shape=(
+            jax.ShapeDtypeStruct((SLOTS, ROWS, 2 * BLOCK_CH), BF),
+            jax.ShapeDtypeStruct((4, 4, 2, 2, STN_DEV, BLOCK_CH), BF),
+            jax.ShapeDtypeStruct((SLOTS, BLOCK_CH), jnp.int32),
+        ),
+        in_specs=[vmem, vmem, vmem, anywhere],
+        out_specs=(anywhere, anywhere, anywhere),
         scratch_shapes=[
             *[pltpu.VMEM((2, 4, 4, UNITS, STN_DEV, BLOCK_CH), BF) for unused in range(4)],
             pltpu.VMEM((3, UNITS, STN_DEV, BLOCK_CH), BF),
             pltpu.VMEM((4, FRAME, 4 * BLOCK_CH), BF),
             pltpu.VMEM((256, BLOCK_CH), F32),
             pltpu.VMEM((SLOTS, ROWS, 2 * BLOCK_CH), BF),
+            pltpu.VMEM((2, 4, 4, 2, STN_DEV, BLOCK_CH), BF),
+            pltpu.VMEM((2, 4, 4, 2, STN_DEV, BLOCK_CH), BF),
+            pltpu.VMEM((4, 2, 4, 2, STN_DEV, BLOCK_CH), BF),
+            pltpu.VMEM((4, 4, 2, 2, STN_DEV, BLOCK_CH), BF),
+            pltpu.VMEM((SLOTS, BLOCK_CH), jnp.int32),
+            pltpu.SMEM((SLOTS, BLOCK_CH), jnp.int32),
             pltpu.SemaphoreType.DMA((4,)),
             pltpu.SemaphoreType.DMA((4,)),
             pltpu.SemaphoreType.DMA((4,)),
             pltpu.SemaphoreType.DMA((4, MESSAGES)),
             pltpu.SemaphoreType.DMA((4, MESSAGES)),
             pltpu.SemaphoreType.DMA((4,)),
+            pltpu.SemaphoreType.DMA((8,)),
+            pltpu.SemaphoreType.DMA((8,)),
+            pltpu.SemaphoreType.DMA((6,)),
         ],
         compiler_params=pltpu.CompilerParams(
             collective_id=0, has_side_effects=True, vmem_limit_bytes=48 * 2**20
         ),
         name="gather_correlate",
-    )(info, filtered, table)
-
-
-def grid_kernel_body(info, count, lists, kernel_t, vis, out, total, weights):
+    )(lists, facts, filtered, table)
+
+
+BATCH = 4
+BATCHES = SLOTS // BATCH + 2
+PIECES = 4
+
+
+def gridding_kernel(
+    info, lists, kernel_t, vis, out, total, weights_a, weights_b, along, tiles, order, used, sems
+):
+    used[0] = 0
+    used[1] = 0
+
+    def clear(s, carry):
+        order[s] = SLOTS
+        return carry
+
+    lax.fori_loop(0, 2 * SLOTS, clear, 0)
+
+    def place(s, carry):
+        @pl.when(info[s, 0] > 0)
+        def _():
+            m = info[s, 2]
+            at = used[m]
+            order[m * SLOTS + at] = s
+            used[m] = at + 1
+
+        return carry
+
+    lax.fori_loop(0, SLOTS, place, 0)
+    first = (used[0] + BATCH - 1) // BATCH
+    batches = first + (used[1] + BATCH - 1) // BATCH
+
+    def member(j, i):
+        m = jnp.where(j >= first, 1, 0)
+        at = (j - m * first) * BATCH + i
+        present = (j < batches) & (at < used[m])
+        s = order[m * SLOTS + jnp.where(present, at, 0)]
+        s = jnp.where(present, s, 0)
+        return present, s, jnp.where(present, info[s, 0], 0)
+
+    def tile_copy(j, i, s):
+        return pltpu.make_async_copy(
+            vis.at[s], tiles.at[j, pl.ds(i * ROWS, ROWS)], sems.at[j]
+        )
+
+    def fetch(j, carry):
+        for i in range(BATCH):
+            present, s, unused_alive = member(j, i)
+
+            @pl.when(present)
+            def _():
+                tile_copy(j, i, s).start()
+
+            @pl.when(jnp.logical_not(present))
+            def _():
+                tiles[j, i * ROWS : (i + 1) * ROWS] = jnp.zeros((ROWS, 2 * BLOCK_CH), BF)
+
+        return carry
+
+    lax.fori_loop(0, batches, fetch, 0)
     total[...] = jnp.zeros_like(total)
+
+    def fetched(j):
+        for i in range(BATCH):
+            present, unused_s, unused_alive = member(j, i)
+
+            @pl.when(present)
+            def _():
+                tile_copy(j, i, 0).wait()
 
     def axis_weight(position, offset):
         chosen = jnp.zeros((8, ROWS), F32)
@@ -343,40 +536,83 @@
             )
         return placed
 
-    def slot(s, carry):
-        m = info[s * 2 + 1]
-        rows = lists[s].astype(jnp.int32)
-        along_x = axis_weight(rows[0:1], rows[2:3])
-        along_y = axis_weight(rows[1:2], rows[3:4])
-        live = lax.broadcasted_iota(jnp.int32, (SIDE, ROWS), 1) < count[s]
-        along_y = jnp.where(live, along_y, 0.0)
-        for v in range(SIDE):
-            weights[v * SIDE : (v + 1) * SIDE] = (
-                along_x * jnp.broadcast_to(along_y[v : v + 1], (SIDE, ROWS))
-            ).astype(BF)
-        total[m] += jnp.dot(weights[...], vis[s], preferred_element_type=F32)
+    def build_axes(j):
+        for i in range(BATCH):
+            unused_present, s, alive = member(j, i)
+            g = s // MOST
+            unit = lists[g % 4, (g // 4) % 4, g // 16, 0].astype(F32).astype(jnp.int32)
+            half = jnp.where(s % MOST == 0, unit[0:8], unit[8:16])
+            rows = [
+                jnp.concatenate([half[2 * q : 2 * q + 1], half[2 * q + 1 : 2 * q + 2]], axis=1)
+                for q in range(4)
+            ]
+            along[i, 0] = axis_weight(rows[0], rows[2])
+            along_y = axis_weight(rows[1], rows[3])
+            live = lax.broadcasted_iota(jnp.int32, (SIDE, ROWS), 1) < alive
+            along[i, 1] = jnp.where(live, along_y, 0.0)
+
+    def build_rows(weights, first_v, last_v):
+        for i in range(BATCH):
+            along_x = along[i, 0]
+            for v in range(first_v, last_v):
+                weights[v * SIDE : (v + 1) * SIDE, i * ROWS : (i + 1) * ROWS] = (
+                    along_x * jnp.broadcast_to(along[i, 1, v : v + 1], (SIDE, ROWS))
+                ).astype(BF)
+
+    def step(j, weights, following):
+        m = jnp.where(j >= first, 1, 0)
+        build_axes(j + 1)
+        span = CELLS // PIECES
+        for q in range(PIECES):
+            cells = slice(q * span, (q + 1) * span)
+            build_rows(following, q * SIDE // PIECES, (q + 1) * SIDE // PIECES)
+            total[m, cells] += jnp.dot(weights[cells], tiles[j], preferred_element_type=F32)
+
+    build_axes(0)
+    build_rows(weights_a, 0, SIDE)
+
+    def pair(i, carry):
+        j = 2 * i
+        fetched(j)
+        step(j, weights_a, weights_b)
+
+        @pl.when(j + 1 < batches)
+        def _():
+            fetched(j + 1)
+            step(j + 1, weights_b, weights_a)
+
         return carry
 
-    lax.fori_loop(0, SLOTS, slot, 0)
+    lax.fori_loop(0, (batches + 1) // 2, pair, 0)
     for m in range(2):
-        out[:, m * 256 : (m + 1) * 256] = total[m] * (1.0 / 32.0)
-
-
-def gridding(info, count, lists, kernel_t, vis):
+        out[:, m, :] = total[m] * (1.0 / 32.0)
+
+
+def gridding(info, lists, kernel_t, vis):
     vmem = pl.BlockSpec(memory_space=pltpu.VMEM)
-    smem = pl.BlockSpec(memory_space=pltpu.SMEM)
     return pl.pallas_call(
-        grid_kernel_body,
-        out_shape=jax.ShapeDtypeStruct((CELLS, 2 * 2 * BLOCK_CH), F32),
-        in_specs=[smem, smem, vmem, vmem, vmem],
+        gridding_kernel,
+        out_shape=jax.ShapeDtypeStruct((CELLS, 2, 2 * BLOCK_CH), F32),
+        in_specs=[
+            pl.BlockSpec(memory_space=pltpu.SMEM),
+            vmem,
+            vmem,
+            pl.BlockSpec(memory_space=pl.ANY),
+        ],
         out_specs=vmem,
         scratch_shapes=[
             pltpu.VMEM((2, CELLS, 2 * BLOCK_CH), F32),
-            pltpu.VMEM((CELLS, ROWS), BF),
+            pltpu.VMEM((CELLS, BATCH * ROWS), BF),
+            pltpu.VMEM((CELLS, BATCH * ROWS), BF),
+            pltpu.VMEM((BATCH, 2, SIDE, ROWS), F32),
+            pltpu.VMEM((BATCHES, BATCH * ROWS, 2 * BLOCK_CH), BF),
+            pltpu.SMEM((2 * SLOTS,), jnp.int32),
+            pltpu.SMEM((2,), jnp.int32),
+            pltpu.SemaphoreType.DMA((BATCHES,)),
         ],
-        compiler_params=pltpu.CompilerParams(vmem_limit_bytes=40 * 2**20),
+        compiler_params=pltpu.CompilerParams(vmem_limit_bytes=56 * 2**20),
         name="gridding",
-    )(info, count, lists, kernel_t, vis)
+    )(info, lists, kernel_t, vis)
 
 
 def polyphase(voltages, filter_taps):
@@ -390,12 +626,13 @@
     return filtered.astype(BF).reshape(frames * by_frame.shape[1], FRAME)
 
 
-def route(uv_corners, kernel_offsets, row_counts, grid_tiles):
+def route_lists(uv_corners, kernel_offsets, row_counts, grid_tiles):
     owners = grid_tiles[0, 0]
     tiles = owners.shape[0]
     tile_ids = jnp.arange(tiles, dtype=jnp.int32)
-    extra = jnp.stack([row_counts[0, 0], tile_ids // 2, tile_ids % 2], axis=1)
-    extra = jnp.pad(extra, ((0, 0), (0, 125)))
+    partner = (lax.axis_index("stn") + tile_ids // 2) % GROUPS
+    extra = jnp.stack([row_counts[0, 0], partner, tile_ids % 2], axis=1)
+    extra = jnp.pad(extra, ((0, 0), (0, BLOCK_CH - 3)))
     packed = jnp.concatenate(
         [uv_corners[0, 0].reshape(tiles, 512), kernel_offsets[0, 0].reshape(tiles, 512), extra],
         axis=1,
@@ -405,23 +642,16 @@
     slot_of = jnp.sum((same & earlier).astype(jnp.int32), axis=1)
     target = owners * MOST + slot_of
     picker = (target[None, :] == jnp.arange(SLOTS, dtype=jnp.int32)[:, None]).astype(BF)
-    send = jnp.dot(picker, packed, preferred_element_type=F32).astype(BF)
-    send = send.reshape(GROUPS, MOST, LISTS + 128)
-    got = lax.all_to_all(send, "stn", split_axis=0, concat_axis=0, tiled=True)
-    got = got.reshape(SLOTS, LISTS + 128)
-    facts = got[:, LISTS : LISTS + 3].astype(jnp.int32)
-    group = jnp.arange(SLOTS, dtype=jnp.int32) // MOST
-    partner = (group + facts[:, 1]) % GROUPS
-    info = jnp.stack([partner, facts[:, 2]], axis=1).reshape(-1)
-    return info, facts[:, 0], got[:, :LISTS].reshape(SLOTS, 4, ROWS).astype(F32)
+    send = jnp.dot(picker, packed, preferred_element_type=F32)
+    lists = send[:, :LISTS].astype(BF).reshape(GROUPS, STN_DEV, BLOCK_CH)
+    return lists, send[:, LISTS:]
 
 
 def on_device(voltages, pfb_taps, grid_kernel, uv_corners, kernel_offsets, row_counts, grid_tiles):
-    info, count, lists = route(uv_corners, kernel_offsets, row_counts, grid_tiles)
+    lists, facts = route_lists(uv_corners, kernel_offsets, row_counts, grid_tiles)
     filtered = polyphase(voltages[:, 0], pfb_taps)
-    vis = gather_and_correlate(info, filtered, jnp.asarray(dft_table()))
-    gridded = gridding(info, count, lists, grid_kernel.T, vis)
-    return gridded.reshape(1, CELLS, 2, 2 * BLOCK_CH)
+    vis, slot_lists, info = gather_and_correlate(lists, facts, filtered, jnp.asarray(dft_table()))
+    return gridding(info, slot_lists, grid_kernel.T, vis)[None]
 
 
 def solution(mesh):

time: 170 us -> 157 us (0.924)
  the two profiles are of different devices: /device:TPU:8 before, /device:TPU:4 now
where the time goes in v2:
time: 157 us
  Pallas kernels  146 us (93%)
  other arithmetic  6.33 us (4%)
  local copies, waits for them, and re-layouts  3.88 us (2%)
    pallas_call x1, Pallas kernels, gather_and_correlate(): pl.pallas_call(gather_kernel, out_shape=(jax.ShapeDtypeStruct((SLOTS, ROW...  120 us
    pallas_call x1, Pallas kernels, gridding(): pl.pallas_call(gridding_kernel, out_shape=jax.ShapeDtypeStruct((CELLS, 2,...  26.6 us

profile of v2, /device:TPU:4, one launch (start us, length us, event | category | flops | bytes accessed | tf_op | source)
XLA Modules:
  0.0 156.9 jit_solution(2067762610061423127)
XLA Ops:
  0.0 0.7 convert_bitcast_fusion.2
  0.7 0.9 convert_reduce_fusion
  1.6 0.7 multiply_add_fusion
  2.3 1.3 copy.12
  3.6 0.1 copy.13
  3.7 0.9 fusion.19
  4.7 0.9 convert_bitcast_fusion.1
  5.6 0.9 convert_bitcast_fusion
  6.6 0.2 fusion.2
  6.8 0.1 reshape.106.lists
  6.9 2.2 %add_convert_fusion = bf16[8,16,2048]{2,1,0:T(8,128)(2,1)S(1)} fusion(bf16[11,16,2048]{2,1,0:T(8,128)(2,1)} %bitcast.25, f32[2048]{0:T(1024)S(1)} %bitcast.32, f32[2048]{0:T(1024)S(1)} %bitcast.33, f32[2048]{0:T(1024)S(1)} %bitcast.31, f32[2048]{0:T(1024)S(1)} %bitcast.30), kind=kLoop, calls=%fused_computation | loop fusion | flops 3145728 | bytes 2654208 | tf_op jit(solution)/shard_map/convert_element_type | solution.py:626
  9.1 119.8 %gather_correlate.1 = (bf16[64,256,256]{2,1,0:T(8,128)(2,1)}, bf16[4,4,2,2,16,128]{5,4,3,2,1,0:T(8,128)(2,1)S(1)}, s32[64,128]{1,0:T(8,128)S(1)}) custom-call(bf16[32,16,128]{2,1,0:T(8,128)(2,1)S(1)} %reshape.106.lists, f32[64,128]{1,0:T(8,128)S(1)} %slice.42.facts, bf16[128,2048]{1,0:T(8,128)(2,1)S(1)} %bitcast.24, bf16[4,2048,512]{2,1,0:T(8,128)(2,1)} %constant.52.clone.table), custom_call_target="tpu_custom_call" | custom-call | tf_op jit(solution)/shard_map/gather_correlate/pallas_call | solution.py:417
  128.9 0.0 copy-start
  128.9 0.7 copy-done
  129.7 0.0 copy-start.1
  129.7 0.6 copy-done.1
  130.3 26.6 %gridding.1 = f32[1024,2,256]{2,1,0:T(2,128)} custom-call(s32[64,128]{1,0:T(8,128)} %copy-done.1, bf16[4,4,2,2,16,128]{5,4,3,2,1,0:T(8,128)(2,1)} %copy-done, f32[8,8]{1,0:T(8,128)} %bitcast.34, bf16[64,256,256]{2,1,0:T(8,128)(2,1)} %get-tuple-element.10.vis), custom_call_target="tpu_custom_call" | custom-call | tf_op jit(solution)/shard_map/gridding/pallas_call | solution.py:593
  (8 shorter events, 0.1 us)
Async XLA Ops:
  128.9 0.7 copy-start
  129.7 0.6 copy-start.1

commit v3 on v2

--- a/solution.py
+++ b/solution.py
@@ -27,10 +27,10 @@
 MESH = pl.DeviceIdType.MESH
 
 UNITS = 32
-A0, A1 = 0, 11
-B0, B1 = 11, 22
-C10, C1M, C11 = 22, 25, 27
-C20, C2M, C21 = 27, 29, 32
+A_ENDS = (11, 10, 11, 10)
+B_END = 21
+C1_CUT, C1_END = 24, 26
+C2_CUT = 29
 MESSAGES = 38
 
 
@@ -48,7 +48,8 @@
 def gather_kernel(
     lists,
     facts,
-    filtered,
+    frames,
+    taps,
     table,
     out,
     out_lists,
@@ -57,6 +58,7 @@
     grp1,
     grp2,
     grp3,
+    filtered,
     held,
     tab,
     rows32,
@@ -133,20 +135,20 @@
         def msg(number, where, dest):
             return (number, message(k, number, where, dest))
 
-        a, b = span(A0, A1), span(B0, B1)
-        c1, c2, c = span(C10, C11), span(C20, C21), span(C10, C21)
+        a, b = span(0, A_ENDS[k]), span(A_ENDS[k], B_END)
+        c1, c2, c = span(B_END, C1_END), span(C1_END, UNITS), span(B_END, UNITS)
         direct1 = [
             msg(1, (y, z, x, c1), "xp"),
             msg(2, (y, z, x, c1), "xm"),
             msg(5, (y, z, x, c2), "zp"),
             msg(6, (y, z, x, c2), "zm"),
-            msg(0, (y, z, x, span(A0, B1)), "y"),
+            msg(0, (y, z, x, span(0, B_END)), "y"),
         ]
         fwd1 = [
-            (1, msg(3, (y, z, xm, span(C10, C1M)), "xp")),
-            (2, msg(4, (y, z, xp, span(C1M, C11)), "xm")),
-            (5, msg(7, (y, zm, x, span(C20, C2M)), "zp")),
-            (6, msg(8, (y, zp, x, span(C2M, C21)), "zm")),
+            (1, msg(3, (y, z, xm, span(B_END, C1_CUT)), "xp")),
+            (2, msg(4, (y, z, xp, span(C1_CUT, C1_END)), "xm")),
+            (5, msg(7, (y, zm, x, span(C1_END, C2_CUT)), "zp")),
+            (6, msg(8, (y, zp, x, span(C2_CUT, UNITS)), "zm")),
         ]
         rest1 = [0, 3, 4, 7, 8]
         direct2 = [
@@ -251,6 +253,15 @@
             device_id={"stn": device},
             device_id_type=MESH,
         )
+
+    for column in range(0, FRAME, 256):
+        columns = slice(column, column + 256)
+        samples = [frames[i, :, columns].astype(F32) for i in range(FR_DEV + TAPS - 1)]
+        for t in range(FR_DEV):
+            value = taps[0:1, columns] * samples[t]
+            for tap in range(1, TAPS):
+                value = value + taps[tap : tap + 1, columns] * samples[t + tap]
+            filtered[t * STN_DEV : (t + 1) * STN_DEV, columns] = value.astype(BF)
 
     pl.semaphore_wait(barrier, 10)
     route_y = route(0, to_send.at[yn], by_y.at[y], to["y"])
@@ -411,7 +422,7 @@
     lists_next.wait()
 
 
-def gather_and_correlate(lists, facts, filtered, table):
+def gather_and_correlate(lists, facts, frames, taps, table):
     vmem = pl.BlockSpec(memory_space=pltpu.VMEM)
     anywhere = pl.BlockSpec(memory_space=pl.ANY)
     return pl.pallas_call(
@@ -421,10 +432,11 @@
             jax.ShapeDtypeStruct((4, 4, 2, 2, STN_DEV, BLOCK_CH), BF),
             jax.ShapeDtypeStruct((SLOTS, BLOCK_CH), jnp.int32),
         ),
-        in_specs=[vmem, vmem, vmem, anywhere],
+        in_specs=[vmem, vmem, vmem, vmem, anywhere],
         out_specs=(anywhere, anywhere, anywhere),
         scratch_shapes=[
             *[pltpu.VMEM((2, 4, 4, UNITS, STN_DEV, BLOCK_CH), BF) for unused in range(4)],
+            pltpu.VMEM((FR_DEV * STN_DEV, FRAME), BF),
             pltpu.VMEM((3, UNITS, STN_DEV, BLOCK_CH), BF),
             pltpu.VMEM((4, FRAME, 4 * BLOCK_CH), BF),
             pltpu.VMEM((256, BLOCK_CH), F32),
@@ -449,25 +461,19 @@
             collective_id=0, has_side_effects=True, vmem_limit_bytes=48 * 2**20
         ),
         name="gather_correlate",
-    )(lists, facts, filtered, table)
-
-
-BATCH = 4
+    )(lists, facts, frames, taps, table)
+
+
+BATCH = 2
 BATCHES = SLOTS // BATCH + 2
 PIECES = 4
 
 
 def gridding_kernel(
-    info, lists, kernel_t, vis, out, total, weights_a, weights_b, along, tiles, order, used, sems
+    info, lists, kernel, vis, out, kernel_t, total, weights_a, weights_b, along, tiles, order, used, sems
 ):
     used[0] = 0
     used[1] = 0
-
-    def clear(s, carry):
-        order[s] = SLOTS
-        return carry
-
-    lax.fori_loop(0, 2 * SLOTS, clear, 0)
 
     def place(s, carry):
         @pl.when(info[s, 0] > 0)
@@ -487,8 +493,7 @@
         m = jnp.where(j >= first, 1, 0)
         at = (j - m * first) * BATCH + i
         present = (j < batches) & (at < used[m])
-        s = order[m * SLOTS + jnp.where(present, at, 0)]
-        s = jnp.where(present, s, 0)
+        s = jnp.where(present, order[m * SLOTS + jnp.where(present, at, 0)], 0)
         return present, s, jnp.where(present, info[s, 0], 0)
 
     def tile_copy(j, i, s):
@@ -512,6 +517,13 @@
 
     lax.fori_loop(0, batches, fetch, 0)
     total[...] = jnp.zeros_like(total)
+    row = lax.broadcasted_iota(jnp.int32, (8, BLOCK_CH), 0)
+    lane = lax.broadcasted_iota(jnp.int32, (8, BLOCK_CH), 1)
+    transposed = jnp.zeros((8, BLOCK_CH), F32)
+    for o in range(8):
+        for k in range(8):
+            transposed = jnp.where((row == k) & (lane == o), kernel[o, k], transposed)
+    kernel_t[...] = transposed
 
     def fetched(j):
         for i in range(BATCH):
@@ -588,7 +600,7 @@
         out[:, m, :] = total[m] * (1.0 / 32.0)
 
 
-def gridding(info, lists, kernel_t, vis):
+def gridding(info, lists, kernel, vis):
     vmem = pl.BlockSpec(memory_space=pltpu.VMEM)
     return pl.pallas_call(
         gridding_kernel,
@@ -596,11 +608,12 @@
         in_specs=[
             pl.BlockSpec(memory_space=pltpu.SMEM),
             vmem,
-            vmem,
+            pl.BlockSpec(memory_space=pltpu.SMEM),
             pl.BlockSpec(memory_space=pl.ANY),
         ],
         out_specs=vmem,
         scratch_shapes=[
+            pltpu.VMEM((8, BLOCK_CH), F32),
             pltpu.VMEM((2, CELLS, 2 * BLOCK_CH), F32),
             pltpu.VMEM((CELLS, BATCH * ROWS), BF),
             pltpu.VMEM((CELLS, BATCH * ROWS), BF),
@@ -612,18 +625,7 @@
         ],
         compiler_params=pltpu.CompilerParams(vmem_limit_bytes=56 * 2**20),
         name="gridding",
-    )(info, lists, kernel_t, vis)
-
-
-def polyphase(voltages, filter_taps):
-    by_frame = jnp.transpose(voltages, (1, 0, 2))
-    frames = by_frame.shape[0] - TAPS + 1
-    filtered = jnp.zeros((frames,) + by_frame.shape[1:], F32)
-    for tap in range(TAPS):
-        filtered = filtered + filter_taps[tap][None, None, :] * by_frame[
-            tap : tap + frames
-        ].astype(F32)
-    return filtered.astype(BF).reshape(frames * by_frame.shape[1], FRAME)
+    )(info, lists, kernel, vis)
 
 
 def route_lists(uv_corners, kernel_offsets, row_counts, grid_tiles):
@@ -649,9 +651,11 @@
 
 def on_device(voltages, pfb_taps, grid_kernel, uv_corners, kernel_offsets, row_counts, grid_tiles):
     lists, facts = route_lists(uv_corners, kernel_offsets, row_counts, grid_tiles)
-    filtered = polyphase(voltages[:, 0], pfb_taps)
-    vis, slot_lists, info = gather_and_correlate(lists, facts, filtered, jnp.asarray(dft_table()))
-    return gridding(info, slot_lists, grid_kernel.T, vis)[None]
+    frames = jnp.transpose(voltages[:, 0], (1, 0, 2))
+    vis, slot_lists, info = gather_and_correlate(
+        lists, facts, frames, pfb_taps, jnp.asarray(dft_table())
+    )
+    return gridding(info, slot_lists, grid_kernel, vis)[None]
 
 
 def solution(mesh):

time: 157 us -> 154 us (0.981)
  the two profiles are of different devices: /device:TPU:4 before, /device:TPU:8 now
where the time goes in v3:
time: 154 us; the launch traced here: 153 us
  Pallas kernels  145 us (94%)
  other arithmetic  4.08 us (3%)
  local copies, waits for them, and re-layouts  3.46 us (2%)
    pallas_call x1, Pallas kernels, gather_and_correlate(): pl.pallas_call(gather_kernel, out_shape=(jax.ShapeDtypeStruct((SLOTS, ROW...  120 us
    pallas_call x1, Pallas kernels, gridding(): pl.pallas_call(gridding_kernel, out_shape=jax.ShapeDtypeStruct((CELLS, 2,...  24.6 us
    unnamed x13, local copies, waits for them, and re-layouts  3.37 us

profile of v3, /device:TPU:8, one launch (start us, length us, event | category | flops | bytes accessed | tf_op | source)
XLA Modules:
  0.0 152.5 jit_solution(3711769462684686259)
XLA Ops:
  0.0 0.7 convert_bitcast_fusion.2
  0.7 0.9 convert_reduce_fusion
  1.6 0.7 multiply_add_fusion
  2.3 0.1 copy.11
  2.4 0.9 convert_bitcast_fusion.1
  3.4 0.9 convert_bitcast_fusion
  4.3 0.2 fusion.2
  4.5 0.1 reshape.99.lists
  4.6 0.0 copy-start
  4.6 1.1 copy-done
  5.7 0.0 copy-start.2
  5.7 0.8 copy-done.2
  6.5 120.1 %gather_correlate.1 = (bf16[64,256,256]{2,1,0:T(8,128)(2,1)}, bf16[4,4,2,2,16,128]{5,4,3,2,1,0:T(8,128)(2,1)S(1)}, s32[64,128]{1,0:T(8,128)S(1)}) custom-call(bf16[32,16,128]{2,1,0:T(8,128)(2,1)S(1)} %reshape.99.lists, f32[64,128]{1,0:T(8,128)S(1)} %slice.10.facts, bf16[11,16,2048]{2,1,0:T(8,128)(2,1)S(1)} %bitcast.18, f32[4,2048]{1,0:T(4,128)S(1)} %copy-done.2, ...), custom_call_target="tpu_custom_call" | custom-call | tf_op jit(solution)/shard_map/gather_correlate/pallas_call | solution.py:428
  126.6 0.0 copy-start.1
  126.6 0.7 copy-done.1
  127.3 0.0 copy-start.3
  127.3 0.6 copy-done.3
  127.9 24.6 %gridding.1 = f32[1024,2,256]{2,1,0:T(2,128)} custom-call(s32[64,128]{1,0:T(8,128)} %copy-done.3, bf16[4,4,2,2,16,128]{5,4,3,2,1,0:T(8,128)(2,1)} %copy-done.1, f32[8,8]{1,0:T(8,128)} %kernel.1, bf16[64,256,256]{2,1,0:T(8,128)(2,1)} %get-tuple-element.10.vis), custom_call_target="tpu_custom_call" | custom-call | tf_op jit(solution)/shard_map/gridding/pallas_call | solution.py:605
  (8 shorter events, 0.1 us)
Async XLA Ops:
  4.6 1.1 copy-start
  5.7 0.8 copy-start.2
  126.6 0.7 copy-start.1
  127.3 0.6 copy-start.3
